TPU v7x, 512 devices: a whole 4x4x16 slice. The times are simulated.
512 devices in a mesh: wide: 128 (over z_lo, x, y, core), narrow: 4 (over z_hi).
Axes of the slice: x: 4, y: 4, z: 16 (z_hi: 4, z_lo: 4; z = z_hi * 4 + z_lo), core: 2. Of those that a mesh axis runs over, the one named last changes fastest.
Arguments:
- grad_in: float32 [131072, 128], P(('wide', 'narrow')), may hold values from -6 to 6
- phi_slope: bfloat16 [131072, 128], P(('wide', 'narrow')), may hold values from 0.049804688 to 1
- activations: bfloat16 [131072, 128], P(('wide', 'narrow')), may hold values from -6 to 6
- weight: bfloat16 [128, 128], replicated, may hold values from -0.5 to 0.5
- local_tiles: bfloat16 [512, 8, 128, 128], P(('wide', 'narrow')), may hold values from -0.0625 to 0.0625
- local_rows: int32 [512, 8], P(('wide', 'narrow')), may hold values from 0 to 1, as said below
- local_cols: int32 [512, 8], P(('wide', 'narrow')), may hold values from 0 to 7, as said below
- local_count: int32 [512], P(('wide', 'narrow')), may hold values from 1 to 8, 3072 in all
- remote_tiles: bfloat16 [512, 112, 128, 128], P(('wide', 'narrow')), may hold values from -0.0625 to 0.0625
- remote_rows: int32 [512, 112], P(('wide', 'narrow')), may hold values from 0 to 1, as said below
- remote_cols: int32 [512, 112], P(('wide', 'narrow')), may hold values from 0 to 55, as said below
- remote_count: int32 [512], P(('wide', 'narrow')), may hold values from 1 to 112, 43008 in all
- send_list: int32 [512, 128, 56], P(('wide', 'narrow')), may hold values from 0 to 1023
Outputs:
- adjoint: float32 [131072, 128], P(('wide', 'narrow'))
- weight_grad: float32 [128, 128], replicated
Inputs may be any that keep to these rules, and one draw needn't show every extreme that they name: `local_count`: each device's live local tile slots; slots from this count onward are ignored, and some device uses all 8. `remote_count`: each device's live remote tile slots; slots from this count onward are ignored, and some device uses all 112. On one device no two local slots have the same pair of local_rows and local_cols. `local_cols`: see local_rows. On one device no two remote slots have the same pair of remote_rows and remote_cols. `remote_cols`: see remote_rows.
All inputs are finite; a program needn't handle non-finite values.
Results may differ from a plain program's by a relative error of at most 0.0031.
Values may be sent and summed in bfloat16 or wider, within the bound.
A program may use at most 64 MiB of HBM per device.

v0:
```python
import jax
import jax.numpy as jnp
from jax import lax
from jax.sharding import PartitionSpec as P

ITERS = 2


GAMMA = 0.5


def row_table(row_ids, live_count, blocks):
    slot_count = row_ids.shape[0]
    is_live = jnp.arange(slot_count, dtype=jnp.int32) < live_count
    matches = row_ids[None, :] == jnp.arange(blocks, dtype=jnp.int32)[:, None]
    return (matches & is_live[None, :]).astype(jnp.float32)


def tile_product(tile_values, table, picked, hidden):
    product = jnp.einsum("kij,kjh->kih", tile_values, picked, preferred_element_type=jnp.float32)
    summed = jnp.einsum("rk,kih->rih", table, product, precision=lax.Precision.HIGHEST)
    return summed.reshape(-1, hidden)


def per_device(
    grad_in,
    phi_slope,
    activations,
    weight,
    local_tiles,
    local_rows,
    local_cols,
    local_count,
    remote_tiles,
    remote_rows,
    remote_cols,
    remote_count,
    send_list,
):
    dev_rows = grad_in.shape[0]
    hidden = grad_in.shape[1]
    tile_size = local_tiles.shape[2]
    blocks = dev_rows // tile_size
    group_blocks = lax.axis_size("narrow") * blocks
    near_table = row_table(local_rows[0], local_count[0], blocks)
    far_table = row_table(remote_rows[0], remote_count[0], blocks)
    all_tiles = jnp.concatenate([local_tiles[0], remote_tiles[0]], axis=0)
    all_table = jnp.concatenate([near_table, far_table], axis=1)
    all_cols = jnp.concatenate([local_cols[0], remote_cols[0] + group_blocks], axis=0)
    adjoint = grad_in
    for iteration in range(ITERS):
        mapped = jnp.einsum(
            "nk,hk->nh", adjoint.astype(jnp.bfloat16), weight, preferred_element_type=jnp.float32
        )
        message = (mapped * phi_slope).astype(jnp.bfloat16)
        gathered = lax.all_gather(message, "narrow", axis=0, tiled=True)
        outgoing = gathered[send_list[0]]
        incoming = lax.all_to_all(outgoing, "wide", split_axis=0, concat_axis=0, tiled=True)
        halo_blocks = incoming.reshape(-1, tile_size, hidden)
        own_blocks = gathered.reshape(-1, tile_size, hidden)
        sources = jnp.concatenate([own_blocks, halo_blocks], axis=0)
        spread = tile_product(all_tiles, all_table, sources[all_cols], hidden)
        adjoint = grad_in + GAMMA * spread
    partial_sum = lax.dot_general(
        activations,
        adjoint.astype(jnp.bfloat16),
        (((0,), (0,)), ((), ())),
        preferred_element_type=jnp.float32,
    )
    summed = lax.psum(partial_sum, ("wide", "narrow"))
    node_total = dev_rows * lax.axis_size("wide") * lax.axis_size("narrow")
    weight_grad = summed * (GAMMA / jnp.sqrt(jnp.float32(node_total)))
    return (adjoint, weight_grad)


def solution(mesh):
    placed = (
        P(("wide", "narrow"), None),
        P(("wide", "narrow"), None),
        P(("wide", "narrow"), None),
        P(),
        P(("wide", "narrow"), None, None, None),
        P(("wide", "narrow"), None),
        P(("wide", "narrow"), None),
        P(("wide", "narrow")),
        P(("wide", "narrow"), None, None, None),
        P(("wide", "narrow"), None),
        P(("wide", "narrow"), None),
        P(("wide", "narrow")),
        P(("wide", "narrow"), None, None),
    )
    return jax.shard_map(
        per_device,
        mesh=mesh,
        in_specs=placed,
        out_specs=(P(("wide", "narrow"), None), P()),
        check_vma=False,
    )
```

profile of v0, /device:TPU:1, one launch (start us, length us, event | category | flops | bytes accessed | tf_op | source)
XLA Modules:
  0.0 687.5 jit_solution(18382776733626664124)
XLA Ops:
  7.2 0.0 copy-start
  7.2 1.1 fusion.12
  8.3 25.3 %all_gather.6 = bf16[1024,128]{1,0:T(8,128)(2,1)S(1)} all-gather(bf16[256,128]{1,0:T(8,128)(2,1)S(1)} %fusion.12), channel_id=1, replica_groups=mesh['wide'=128,'narrow'=4] {'narrow'}, dimensions={0}, use_global_device_ids=true | all-gather | bytes 327680 | tf_op jit(solution)/shard_map/all_gather | solution.py:56
  33.6 0.8 compare_select_fusion
  34.3 0.1 copy.16
  34.4 0.1 reshape.145
  34.5 0.0 copy-start.8
  34.6 0.0 copy-start.9
  34.6 25.5 %gather_fusion = bf16[7168,128]{1,0:T(8,128)(2,1)} fusion(bf16[1024,128]{1,0:T(8,128)(2,1)S(1)} %all_gather.6, s32[7168]{0:T(1024)S(1)} %broadcast_clamp_fusion), kind=kCustom, calls=%fused_computation | custom fusion | bytes 3698688 | tf_op jit(solution)/shard_map/gather | solution.py:57
  60.1 13.1 %all-to-all-start = ((bf16[128,56,128]{2,1,0:T(8,128)(2,1)}), bf16[128,56,128]{2,1,0:T(8,128)(2,1)S(1)}, u32[]{:S(2)}, u32[]{:S(2)}) async-start(bf16[128,56,128]{2,1,0:T(8,128)(2,1)} %bitcast.47), calls=%async_computation | async-start | bytes 3670016 | tf_op jit(solution)/shard_map/all_to_all | solution.py:58
  73.3 0.2 all-reduce.2.cloned.1.call-start
  74.9 0.1 fusion.17
  75.0 44.7 %all-to-all-done = bf16[128,56,128]{2,1,0:T(8,128)(2,1)S(1)} async-done(((bf16[128,56,128]{2,1,0:T(8,128)(2,1)}), bf16[128,56,128]{2,1,0:T(8,128)(2,1)S(1)}, u32[]{:S(2)}, u32[]{:S(2)}) %all-to-all-start) | async-done | bytes 1835040 | tf_op jit(solution)/shard_map/all_to_all | solution.py:58
  119.7 1.3 copy-done.1
  120.9 1.7 pad_maximum_fusion.3
  122.6 2.9 gather_fusion.1
  125.6 4.4 fusion.5
  130.0 7.1 %fusion.6 = f32[2,128,128]{2,0,1:T(2,128)S(1)} fusion(f32[120,128,128]{2,1,0:T(8,128)S(1)} %fusion.5, pred[2,112]{1,0:T(4,128)(4,1)S(1)} %compare_and_fusion, pred[2,8]{1,0:T(4,128)(4,1)S(1)} %compare_and_fusion.1), kind=kOutput, calls=%fused_computation.13 | convolution fusion | flops 47218928 | bytes 7995632 | tf_op jit(solution)/shard_map/rk,kih->rih/dot_general | solution.py:21
  137.1 0.2 fusion.13
  137.3 18.2 %all_gather.7 = bf16[1024,128]{1,0:T(8,128)(2,1)S(1)} all-gather(bf16[256,128]{1,0:T(8,128)(2,1)S(1)} %fusion.13), channel_id=1, replica_groups=mesh['wide'=128,'narrow'=4] {'narrow'}, dimensions={0}, use_global_device_ids=true | all-gather | bytes 327680 | tf_op jit(solution)/shard_map/all_gather | solution.py:56
  155.5 21.1 %gather_fusion.2 = bf16[7168,128]{1,0:T(8,128)(2,1)S(1)} fusion(bf16[1024,128]{1,0:T(8,128)(2,1)S(1)} %all_gather.7, s32[7168]{0:T(1024)S(1)} %broadcast_clamp_fusion), kind=kCustom, calls=%fused_computation.2 | custom fusion | bytes 3698688 | tf_op jit(solution)/shard_map/gather | solution.py:57
  176.6 53.6 %all_to_all.10 = bf16[128,56,128]{2,1,0:T(8,128)(2,1)S(1)} all-to-all(bf16[128,56,128]{2,1,0:T(8,128)(2,1)S(1)} %bitcast.48), channel_id=1, replica_groups=mesh['wide'=128,'narrow'=4] {'wide'}, dimensions={0} | all-to-all | bytes 3670016 | tf_op jit(solution)/shard_map/all_to_all | solution.py:58
  230.2 0.2 pad_maximum_fusion.4
  230.4 2.9 gather_fusion.3
  233.3 4.4 fusion.4
  237.8 7.1 %fusion.9 = f32[2,128,128]{2,0,1:T(2,128)S(1)} fusion(f32[120,128,128]{2,1,0:T(8,128)S(1)} %fusion.4, pred[2,112]{1,0:T(4,128)(4,1)S(1)} %compare_and_fusion, pred[2,8]{1,0:T(4,128)(4,1)S(1)} %compare_and_fusion.1), kind=kOutput, calls=%fused_computation.14 | convolution fusion | flops 47218928 | bytes 7995632 | tf_op jit(solution)/shard_map/rk,kih->rih/dot_general | solution.py:21
  244.9 0.0 copy-start.4
  244.9 0.8 convolution_bitcast_fusion
  245.7 0.0 all-reduce.2.cloned.1.call-update
  245.7 433.4 %all-reduce.2.cloned.1.call-done = f32[128,128]{0,1:T(8,128)} async-done(((f32[128,128]{0,1:T(8,128)}), f32[128,128]{0,1:T(8,128)}) %all-reduce.2.cloned.1.call-update) | async-done | bytes 65552 | tf_op jit(solution)/shard_map/psum | solution.py:70
  679.1 0.8 broadcast_multiply_fusion
  680.0 0.7 copy.19
  (28 shorter events, 0.2 us)
Async XLA Ops:
  7.2 237.7 %copy-start = (bf16[256,128]{1,0:T(8,128)(2,1)S(1)}, bf16[256,128]{1,0:T(8,128)(2,1)}, u32[]{:S(2)}) copy-start(bf16[256,128]{1,0:T(8,128)(2,1)} %param.15) | copy-start | bytes 196612
  34.5 40.3 %copy-start.7 = (s32[1,112]{1,0:T(1,128)S(1)}, s32[1,112]{1,0:T(1,128)}, u32[]{:S(2)}) copy-start(s32[1,112]{1,0:T(1,128)} %param.23) | copy-start | bytes 1348
  34.5 40.3 %copy-start.8 = (s32[1,8]{1,0:T(1,128)S(1)}, s32[1,8]{1,0:T(1,128)}, u32[]{:S(2)}) copy-start(s32[1,8]{1,0:T(1,128)} %param.19) | copy-start | bytes 100
  34.6 40.4 %copy-start.9 = (s32[1,112]{1,0:T(1,128)S(1)}, s32[1,112]{1,0:T(1,128)}, u32[]{:S(2)}) copy-start(s32[1,112]{1,0:T(1,128)} %param.22) | copy-start | bytes 1348
  34.6 40.4 %copy-start.10 = (s32[1,8]{1,0:T(1,128)S(1)}, s32[1,8]{1,0:T(1,128)}, u32[]{:S(2)}) copy-start(s32[1,8]{1,0:T(1,128)} %param.18) | copy-start | bytes 100
  60.1 59.5 %all-to-all-start = ((bf16[128,56,128]{2,1,0:T(8,128)(2,1)}), bf16[128,56,128]{2,1,0:T(8,128)(2,1)S(1)}, u32[]{:S(2)}, u32[]{:S(2)}) async-start(bf16[128,56,128]{2,1,0:T(8,128)(2,1)} %bitcast.47), calls=%async_computation | async-start | bytes 3670016 | tf_op jit(solution)/shard_map/all_to_all | solution.py:58
  73.3 605.8 %all-reduce.2.cloned.1.call-start = ((), (), s32[]{:S(2)}) async-start(), calls=%async_computation.2 | async-start | bytes 131072 | tf_op jit(solution)/shard_map/psum | solution.py:70
  119.7 1.3 copy-start.1
  122.6 2.9 copy-start.3
  130.0 7.1 %copy-start.2 = (f32[256,128]{1,0:T(8,128)S(1)}, f32[256,128]{1,0:T(8,128)}, u32[]{:S(2)}) copy-start(f32[256,128]{1,0:T(8,128)} %param.13) | copy-start | bytes 393220
  130.0 7.1 %copy-start.5 = (bf16[256,128]{1,0:T(8,128)(2,1)S(1)}, bf16[256,128]{1,0:T(8,128)(2,1)}, u32[]{:S(2)}) copy-start(bf16[256,128]{1,0:T(8,128)(2,1)} %param.14) | copy-start | bytes 196612
  130.0 7.1 %copy-start.6 = (bf16[128,128]{1,0:T(8,128)(2,1)S(1)}, bf16[128,128]{1,0:T(8,128)(2,1)}, u32[]{:S(2)}) copy-start(bf16[128,128]{1,0:T(8,128)(2,1)} %param.16) | copy-start | bytes 98308
  244.9 435.8 %copy-start.4 = (f32[256,128]{1,0:T(8,128)}, f32[256,128]{1,0:T(8,128)S(1)}, u32[]{:S(2)}) copy-start(f32[256,128]{1,0:T(8,128)S(1)} %bitcast_add_fusion) | copy-start | bytes 393220
Sparse Core Ops, SparseCore 0:
  245.8 433.2 all-reduce.1
where the time goes:
time: 688 us
  waiting for transfers between devices  478 us (69%)
  blocking collectives  97.1 us (14%)
  local copies, waits for them, and re-layouts  54.7 us (8%)
  matrix products  25.1 us (4%)
  between operations  15.6 us (2%)
  starting transfers between devices  13.4 us (2%)
    psum x1, waiting for transfers between devices, per_device(): summed = lax.psum(partial_sum, ('wide', 'narrow'))  433 us
    all_to_all x1, blocking collectives, per_device(): lax.all_to_all(outgoing, 'wide', split_axis=0, concat_axis=0, tiled=True)  53.6 us
    gather x2, local copies, waits for them, and re-layouts, per_device(): outgoing = gathered[send_list[0]]  46.6 us
    all_to_all x1, waiting for transfers between devices, per_device(): lax.all_to_all(outgoing, 'wide', split_axis=0, concat_axis=0, tiled=True)  44.7 us
    all_gather x2, blocking collectives, per_device(): gathered = lax.all_gather(message, 'narrow', axis=0, tiled=True)  43.5 us
    dot_general x2, matrix products, tile_product(): jnp.einsum('rk,kih->rih', table, product, precision=lax.Precision.HIGHEST)  14.1 us
  transfers between devices with their start and end apart: 2, of which 2 were waited for; matrix products, arithmetic and copies ran while one was open for 0% of the time, Pallas kernels for 0%

commit v1 on v0

v1 whole, which is shorter than its diff:
```python
import functools
import math

import jax
import jax.numpy as jnp
from jax import lax
from jax.experimental import pallas as pl
from jax.experimental.pallas import tpu as pltpu
from jax.sharding import PartitionSpec as P

ITERS = 2
GAMMA = 0.5
Z_LO = 4
CORES = 2
MESH = pl.DeviceIdType.MESH
F32 = jnp.float32
BF16 = jnp.bfloat16


def loop(count, body, start=0):
    def step(i, carry):
        body(i)
        return carry

    lax.fori_loop(start, count, step, 0)


def kernel(
    cfg,
    slot_of,
    grad_ref,
    phi_ref,
    act_ref,
    weight_ref,
    list_ref,
    local_hbm,
    remote_hbm,
    adj_ref,
    wg_ref,
    tiles,
    table,
    lists,
    index,
    picked,
    send,
    recv,
    halo,
    total,
    part,
    plane_sum,
    column_sum,
    wg_all,
    tile_sem,
    list_send,
    list_recv,
    ring_send,
    ring_recv,
    swap_send,
    swap_recv,
    plane_send,
    plane_recv,
    column_send,
    column_recv,
    last_send,
    last_recv,
):
    plane, narrow, rows, tb, sendn, batch, scale = cfg
    depth = Z_LO * narrow
    chips = plane // CORES
    half = rows // 2
    steps = depth // 2
    hidden = grad_ref.shape[1]
    n_local, n_remote = local_hbm.shape[0], remote_hbm.shape[0]
    zero_slot = n_local + n_remote
    blocks = rows // tb
    group_blocks = narrow * blocks
    halo_blocks = halo.shape[0] // tb

    wide_at, narrow_at = lax.axis_index("wide"), lax.axis_index("narrow")
    low, me = wide_at // plane, lax.rem(wide_at, plane)
    z = narrow_at * Z_LO + low
    core = lax.rem(me, CORES)
    chip = me // CORES

    def in_plane(other):
        return (low * plane + other, narrow_at)

    def in_column(other):
        return (lax.rem(other, Z_LO) * plane + me, other // Z_LO)

    def ahead(k):
        return lax.rem(me + k, plane)

    def behind(k):
        return lax.rem(me + plane - k, plane)

    barrier = pltpu.get_barrier_semaphore()

    def greet_plane(k):
        pl.semaphore_signal(barrier, inc=1, device_id=in_plane(ahead(k)), device_id_type=MESH)

    def greet_column(k):
        pl.semaphore_signal(barrier, inc=1, device_id=in_column(lax.rem(z + k, depth)), device_id_type=MESH)

    loop(plane, greet_plane, 1)
    loop(depth, greet_column, 1)

    near_tiles = pltpu.make_async_copy(local_hbm, tiles.at[pl.ds(0, n_local)], tile_sem.at[0])
    far_tiles = pltpu.make_async_copy(remote_hbm, tiles.at[pl.ds(n_local, n_remote)], tile_sem.at[1])
    near_tiles.start()
    far_tiles.start()
    tiles[zero_slot] = jnp.zeros((tb, tb), BF16)

    def make_message(it, adjoint):
        mapped = lax.dot_general(
            adjoint.astype(BF16), weight_ref[...], (((1,), (1,)), ((), ())), preferred_element_type=F32
        )
        message = (mapped * phi_ref[...].astype(F32)).astype(BF16)
        table[it, low, pl.ds(pl.multiple_of(narrow_at * rows, rows), rows), :] = message

    make_message(0, grad_ref[...])
    lists[low] = list_ref[pl.ds(pl.multiple_of(low * plane, 8), plane), :]

    pl.semaphore_wait(barrier, plane - 1 + depth - 1)

    def list_copy(k):
        other = lax.rem(low + k, Z_LO)
        return pltpu.make_async_remote_copy(
            src_ref=list_ref.at[pl.ds(pl.multiple_of(other * plane, 8), plane)],
            dst_ref=lists.at[low],
            send_sem=list_send.at[k],
            recv_sem=list_recv.at[k],
            device_id=(other * plane + me, narrow_at),
            device_id_type=MESH,
        )

    def ring_copy(it, way, step, piece):
        owner = lax.rem(z + (depth - step if way == 0 else step), depth)
        at = pl.multiple_of(owner // Z_LO * rows + piece * half, half)
        ref = table.at[it, lax.rem(owner, Z_LO), pl.ds(at, half)]
        return pltpu.make_async_remote_copy(
            src_ref=ref,
            dst_ref=ref,
            send_sem=ring_send.at[it, way, step, piece],
            recv_sem=ring_recv.at[it, way, step, piece],
            device_id=in_column(lax.rem(z + (1 if way == 0 else depth - 1), depth)),
            device_id_type=MESH,
        )

    def ring_hops():
        for step in range(steps):
            for piece in range(2):
                for way in range(2):
                    if step < steps - 1 or piece == way:
                        yield way, step, piece

    def make_index(source):
        turned = jnp.transpose(lists[source])
        for k in range(plane):
            index[k, source * sendn : (source + 1) * sendn, :] = jnp.broadcast_to(turned[:, k : k + 1], (sendn, 128))

    def gather_column(it):
        for way, step, piece in ring_hops():
            if step == 0:
                ring_copy(it, way, 0, piece).start()

        @pl.when(it == 0)
        def _():
            loop(Z_LO, lambda k: list_copy(k).start(), 1)

        for way, step, piece in ring_hops():
            ring_copy(it, way, step, piece).wait_recv()
            if step < steps - 2 or (step == steps - 2 and piece == way):
                ring_copy(it, way, step + 1, piece).start()
            if step == 0 and way == 1 and piece == 1:

                @pl.when(it == 0)
                def _():
                    loop(Z_LO, lambda k: list_copy(k).wait(), 1)
                    for source in range(Z_LO):
                        make_index(source)

        for way, step, piece in ring_hops():
            ring_copy(it, way, step, piece).wait_send()

    def swap_copy(it, k):
        return pltpu.make_async_remote_copy(
            src_ref=send.at[it, k],
            dst_ref=recv.at[it, k],
            send_sem=swap_send.at[it, k],
            recv_sem=swap_recv.at[it, k],
            device_id=in_plane(ahead(k)),
            device_id_type=MESH,
        )

    group_rows = narrow * rows

    def send_batch(it, first):
        def select(source):
            wanted = jnp.concatenate(
                [index[ahead(first + j), pl.ds(pl.multiple_of(source * sendn, 8), sendn), :] for j in range(batch)], axis=0
            )
            lane = lax.broadcasted_iota(jnp.int32, wanted.shape, 1)
            hot = jnp.concatenate(
                [jnp.where(wanted == lane + at, 1.0, 0.0).astype(BF16) for at in range(0, group_rows, 128)], axis=1
            )
            got = jnp.dot(hot, table[it, source], preferred_element_type=F32)
            for j in range(batch):
                picked[j, pl.ds(pl.multiple_of(source * sendn, 8), sendn), :] = got[j * sendn : (j + 1) * sendn]

        loop(Z_LO, select)

        def post(j):
            send[it, first + j] = picked[j].astype(BF16)

            @pl.when(first + j > 0)
            def _():
                swap_copy(it, first + j).start()

        loop(batch, post)

    def place(it, k, ref):
        got = ref[it, k].astype(F32)
        for source in range(Z_LO):
            at = pl.multiple_of((source * plane + behind(k)) * sendn, 8)
            halo[pl.ds(at, sendn), :] = got[source * sendn : (source + 1) * sendn]

    def tile_pair(base, per_row, c):
        top = jnp.concatenate([tiles[slot_of[base + c]], tiles[slot_of[base + c + 1]]], axis=1)
        low_row = jnp.concatenate(
            [tiles[slot_of[base + per_row + c]], tiles[slot_of[base + per_row + c + 1]]], axis=1
        )
        return jnp.concatenate([top, low_row], axis=0)

    def iterate(it):
        gather_column(it)
        loop(plane // batch, lambda c: send_batch(it, c * batch))
        place(it, 0, send)

        @pl.when(it == 0)
        def _():
            near_tiles.wait()
            far_tiles.wait()

        total[...] = jnp.zeros_like(total)

        def near(c):
            source = table[it, low, pl.ds(pl.multiple_of(c * 2 * tb, tb), 2 * tb), :]
            total[...] += jnp.dot(tile_pair(0, group_blocks, 2 * c), source, preferred_element_type=F32)

        loop(group_blocks // 2, near)

        def receive(k):
            swap_copy(it, k).wait_recv()
            place(it, k, recv)

        loop(plane, receive, 1)

        def far(c):
            source = halo[pl.ds(pl.multiple_of(c * 2 * tb, tb), 2 * tb), :].astype(BF16)
            total[...] += jnp.dot(
                tile_pair(blocks * group_blocks, halo_blocks, 2 * c), source, preferred_element_type=F32
            )

        loop(halo_blocks // 2, far)
        loop(plane, lambda k: swap_copy(it, k).wait_send(), 1)
        adj_ref[...] = grad_ref[...] + GAMMA * total[...]

        @pl.when(it < ITERS - 1)
        def _():
            make_message(it + 1, adj_ref[...])

    loop(ITERS, iterate)

    gradient = lax.dot_general(
        act_ref[...], adj_ref[...].astype(BF16), (((0,), (0,)), ((), ())), preferred_element_type=F32
    )
    piece_rows = hidden // chips
    for j in range(chips):
        part[j] = gradient[j * piece_rows : (j + 1) * piece_rows]

    def plane_copy(k):
        return pltpu.make_async_remote_copy(
            src_ref=part.at[ahead(k) // CORES],
            dst_ref=plane_sum.at[me],
            send_sem=plane_send.at[k],
            recv_sem=plane_recv.at[k],
            device_id=in_plane(ahead(k)),
            device_id_type=MESH,
        )

    loop(plane, lambda k: plane_copy(k).start(), 1)
    plane_sum[me] = part[chip]
    loop(plane, lambda k: plane_copy(k).wait(), 1)
    column_sum[z] = jnp.sum(plane_sum[...], axis=0)

    def column_copy(k):
        return pltpu.make_async_remote_copy(
            src_ref=column_sum.at[z],
            dst_ref=column_sum.at[z],
            send_sem=column_send.at[k],
            recv_sem=column_recv.at[k],
            device_id=in_column(lax.rem(z + k, depth)),
            device_id_type=MESH,
        )

    loop(depth, lambda k: column_copy(k).start(), 1)
    loop(depth, lambda k: column_copy(k).wait(), 1)
    wg_all[chip] = jnp.sum(column_sum[...], axis=0) * scale

    def last_copy(k):
        return pltpu.make_async_remote_copy(
            src_ref=wg_all.at[chip],
            dst_ref=wg_all.at[chip],
            send_sem=last_send.at[k],
            recv_sem=last_recv.at[k],
            device_id=in_plane(ahead(k * CORES)),
            device_id_type=MESH,
        )

    loop(chips, lambda k: last_copy(k).start(), 1)
    loop(chips, lambda k: last_copy(k).wait(), 1)
    wg_ref[...] = wg_all[...]


def slot_table(local_rows, local_cols, local_count, remote_rows, remote_cols, remote_count, blocks, group_blocks, halo_blocks):
    n_local, n_remote = local_rows.shape[0], remote_rows.shape[0]
    near = jnp.where(jnp.arange(n_local) < local_count, local_rows * group_blocks + local_cols, -1)
    far = jnp.where(
        jnp.arange(n_remote) < remote_count, blocks * group_blocks + remote_rows * halo_blocks + remote_cols, -1
    )
    keys = jnp.concatenate([near, far])
    none = n_local + n_remote
    pairs = jnp.arange(blocks * (group_blocks + halo_blocks), dtype=jnp.int32)
    slots = jnp.arange(none, dtype=jnp.int32)
    return none + jnp.sum(jnp.where(keys[None, :] == pairs[:, None], slots[None, :] - none, 0), axis=1)


def per_device(
    grad_in,
    phi_slope,
    activations,
    weight,
    local_tiles,
    local_rows,
    local_cols,
    local_count,
    remote_tiles,
    remote_rows,
    remote_cols,
    remote_count,
    send_list,
):
    wide, narrow = lax.axis_size("wide"), lax.axis_size("narrow")
    plane = wide // Z_LO
    chips = plane // CORES
    depth = Z_LO * narrow
    rows, hidden = grad_in.shape
    tb = local_tiles.shape[2]
    sendn = send_list.shape[2]
    n_local, n_remote = local_tiles.shape[1], remote_tiles.shape[1]
    blocks, group_blocks, halo_blocks = rows // tb, narrow * rows // tb, wide * sendn // tb
    batch = math.gcd(plane, 8)
    scale = GAMMA / math.sqrt(rows * wide * narrow)
    slot_of = slot_table(
        local_rows[0], local_cols[0], local_count[0], remote_rows[0], remote_cols[0], remote_count[0],
        blocks, group_blocks, halo_blocks,
    )
    vmem = pl.BlockSpec(memory_space=pltpu.VMEM)
    anywhere = pl.BlockSpec(memory_space=pl.ANY)
    piece = (hidden // chips, hidden)
    per_dest = Z_LO * sendn
    dma = pltpu.SemaphoreType.DMA
    adjoint, weight_grad = pl.pallas_call(
        functools.partial(kernel, (plane, narrow, rows, tb, sendn, batch, scale)),
        out_shape=(
            jax.ShapeDtypeStruct((rows, hidden), F32),
            jax.ShapeDtypeStruct((chips,) + piece, F32),
        ),
        in_specs=[pl.BlockSpec(memory_space=pltpu.SMEM)] + [vmem] * 5 + [anywhere] * 2,
        out_specs=(vmem, vmem),
        scratch_shapes=[
            pltpu.VMEM((n_local + n_remote + 1, tb, tb), BF16),
            pltpu.VMEM((ITERS, Z_LO, narrow * rows, hidden), BF16),
            pltpu.VMEM((Z_LO, plane, sendn), jnp.int32),
            pltpu.VMEM((plane, per_dest, 128), jnp.int32),
            pltpu.VMEM((batch, per_dest, hidden), F32),
            pltpu.VMEM((ITERS, plane, per_dest, hidden), BF16),
            pltpu.VMEM((ITERS, plane, per_dest, hidden), BF16),
            pltpu.VMEM((wide * sendn, hidden), F32),
            pltpu.VMEM((rows, hidden), F32),
            pltpu.VMEM((chips,) + piece, F32),
            pltpu.VMEM((plane,) + piece, F32),
            pltpu.VMEM((depth,) + piece, F32),
            pltpu.VMEM((chips,) + piece, F32),
            dma((2,)),
            dma((Z_LO,)),
            dma((Z_LO,)),
            dma((ITERS, 2, depth // 2, 2)),
            dma((ITERS, 2, depth // 2, 2)),
            dma((ITERS, plane)),
            dma((ITERS, plane)),
            dma((plane,)),
            dma((plane,)),
            dma((depth,)),
            dma((depth,)),
            dma((chips,)),
            dma((chips,)),
        ],
        compiler_params=pltpu.CompilerParams(
            collective_id=0, has_side_effects=True, vmem_limit_bytes=48 * 1024 * 1024
        ),
    )(slot_of, grad_in, phi_slope, activations, weight, send_list[0], local_tiles[0], remote_tiles[0])
    return adjoint, weight_grad.reshape(hidden, hidden)


def solution(mesh):
    placed = (
        P(("wide", "narrow"), None),
        P(("wide", "narrow"), None),
        P(("wide", "narrow"), None),
        P(),
        P(("wide", "narrow"), None, None, None),
        P(("wide", "narrow"), None),
        P(("wide", "narrow"), None),
        P(("wide", "narrow")),
        P(("wide", "narrow"), None, None, None),
        P(("wide", "narrow"), None),
        P(("wide", "narrow"), None),
        P(("wide", "narrow")),
        P(("wide", "narrow"), None, None),
    )
    return jax.shard_map(
        per_device,
        mesh=mesh,
        in_specs=placed,
        out_specs=(P(("wide", "narrow"), None), P()),
        check_vma=False,
    )
```

time: 688 us -> 163 us (0.24)
  waiting for transfers between devices: 478 us -> 0 us
  Pallas kernels: 0 us -> 151 us
  blocking collectives: 97.1 us -> 0 us
  local copies, waits for them, and re-layouts: 54.7 us -> 8.45 us
  matrix products: 25.1 us -> 0 us
  between operations: 15.6 us -> 1.95 us
  starting transfers between devices: 13.4 us -> 0 us
    psum x1 -> x0, waiting for transfers between devices: 433 us -> none  [per_device(): summed = lax.psum(partial_sum, ('wide', 'narrow'))]
    pallas_call x0 -> x1, Pallas kernels: none -> 151 us  [per_device(): pl.pallas_call(functools.partial(kernel, (plane, narrow, rows, tb, sendn,...]
    all_to_all x1 -> x0, blocking collectives: 53.6 us -> none  [per_device(): lax.all_to_all(outgoing, 'wide', split_axis=0, concat_axis=0, tiled=True)]
    gather x4 -> x0, local copies, waits for them, and re-layouts: 52.5 us -> none  [the longest x2 46.6 us: per_device(): outgoing = gathered[send_list[0]]]
    all_to_all x1 -> x0, waiting for transfers between devices: 44.7 us -> none  [per_device(): lax.all_to_all(outgoing, 'wide', split_axis=0, concat_axis=0, tiled=True)]
    all_gather x2 -> x0, blocking collectives: 43.5 us -> none  [per_device(): gathered = lax.all_gather(message, 'narrow', axis=0, tiled=True)]
    dot_general x7 -> x0, matrix products: 25.1 us -> none  [the longest x2 14.1 us: tile_product(): jnp.einsum('rk,kih->rih', table, product, precision=lax.Precision.HIGHEST)]
    all_to_all x1 -> x0, starting transfers between devices: 13.1 us -> none  [per_device(): lax.all_to_all(outgoing, 'wide', split_axis=0, concat_axis=0, tiled=True)]
  transfers between devices with their start and end apart: 2 -> 0, of which waited for: 2 -> 0; matrix products, arithmetic and copies ran while one was open for 0% -> 0% of each run, Pallas kernels for 0% -> 0%
where the time goes in v1:
time: 163 us
  Pallas kernels  151 us (93%)
  local copies, waits for them, and re-layouts  8.45 us (5%)
  between operations  1.95 us (1%)
    pallas_call x1, Pallas kernels, per_device(): pl.pallas_call(functools.partial(kernel, (plane, narrow, rows, tb, sendn,...  151 us
    unnamed x15, local copies, waits for them, and re-layouts  8.45 us

profile of v1, /device:TPU:1, one launch (start us, length us, event | category | flops | bytes accessed | tf_op | source)
XLA Modules:
  0.0 162.8 jit_solution(4535719335722059330)
XLA Ops:
  1.9 0.7 compare_select_fusion
  2.6 0.7 compare_select_fusion.1
  3.3 0.1 pad_add_fusion
  3.4 0.1 select_reduce_fusion
  3.5 0.8 copy.16
  4.3 0.0 copy-start
  4.3 2.0 %copy-done = bf16[1,112,128,128]{3,2,1,0:T(8,128)(2,1)S(1)} copy-done((bf16[1,112,128,128]{3,2,1,0:T(8,128)(2,1)S(1)}, bf16[1,112,128,128]{3,2,1,0:T(8,128)(2,1)}, u32[]{:S(2)}) %copy-start) | copy-done | bytes 3670040
  6.4 0.0 copy-start.1
  6.4 0.9 copy-done.1
  7.3 0.0 copy-start.2
  7.3 0.9 copy-done.2
  8.2 0.0 copy-start.3
  8.2 0.8 copy-done.3
  9.1 0.0 copy-start.4
  9.1 0.8 copy-done.4
  9.9 0.0 copy-start.5
  9.9 0.8 copy-done.5
  10.7 150.8 %shard_map.140 = (f32[256,128]{1,0:T(8,128)S(1)}, f32[16,8,128]{2,1,0:T(8,128)S(1)}) custom-call(s32[128]{0:T(128)S(1)} %broadcast_add_fusion.slot_of, f32[256,128]{1,0:T(8,128)S(1)} %copy-done.2, bf16[256,128]{1,0:T(8,128)(2,1)S(1)} %copy-done.3, bf16[256,128]{1,0:T(8,128)(2,1)S(1)} %copy-done.4, bf16[128,128]{1,0:T(8,128)(2,1)S(1)} %copy-done.5, ...), custom_call_target="tpu_custom_call" | custom-call | tf_op jit(solution)/shard_map/pallas_call | solution.py:374
  161.5 0.7 copy.21
  162.2 0.6 copy.22
  (1 shorter events, 0.0 us)
Async XLA Ops:
  4.3 2.0 %copy-start = (bf16[1,112,128,128]{3,2,1,0:T(8,128)(2,1)S(1)}, bf16[1,112,128,128]{3,2,1,0:T(8,128)(2,1)}, u32[]{:S(2)}) copy-start(bf16[1,112,128,128]{3,2,1,0:T(8,128)(2,1)} %param.21) | copy-start | bytes 11010052
  6.4 0.9 copy-start.1
  7.3 0.9 copy-start.2
  8.2 0.8 copy-start.3
  9.1 0.8 copy-start.4
  9.9 0.8 copy-start.5

commit v2 on v0

v2 whole, which is shorter than its diff:
```python
import functools
import math

import jax
import jax.numpy as jnp
from jax import lax
from jax.experimental import pallas as pl
from jax.experimental.pallas import tpu as pltpu
from jax.sharding import PartitionSpec as P

ITERS = 2
GAMMA = 0.5
Z_LO = 4
CORES = 2
MESH = pl.DeviceIdType.MESH
F32 = jnp.float32
BF16 = jnp.bfloat16


def loop(count, body, start=0):
    def step(i, carry):
        body(i)
        return carry

    lax.fori_loop(start, count, step, 0)


def kernel(
    cfg,
    local_count,
    remote_count,
    grad_hbm,
    phi_hbm,
    act_hbm,
    weight_hbm,
    list_hbm,
    local_hbm,
    remote_hbm,
    local_rows,
    local_cols,
    remote_rows,
    remote_cols,
    adj_ref,
    wg_ref,
    grad_ref,
    phi_ref,
    act_ref,
    weight_ref,
    list_ref,
    tiles,
    local_at,
    remote_at,
    slot_rows,
    slot_of,
    table,
    lists,
    index,
    send,
    halo,
    total,
    part,
    plane_sum,
    near_sum,
    low_sum,
    wg_all,
    in_sem,
    slot_sem,
    list_send,
    list_recv,
    group_send,
    group_recv,
    twin_send,
    twin_recv,
    swap_send,
    swap_recv,
    plane_send,
    plane_recv,
    near_send,
    near_recv,
    low_send,
    low_recv,
    last_send,
    last_recv,
):
    plane, narrow, rows, tb, sendn, batch, scale = cfg
    depth = Z_LO * narrow
    chips = plane // CORES
    side = math.isqrt(chips)
    count = Z_LO * chips
    per_chip = CORES * sendn
    hidden = grad_ref.shape[1]
    n_local, n_remote = local_hbm.shape[0], remote_hbm.shape[0]
    zero_slot = n_local + n_remote
    blocks = rows // tb
    group_rows = narrow * rows
    group_blocks = narrow * blocks
    layer_blocks = chips * per_chip // tb
    halo_blocks = Z_LO * layer_blocks
    span = math.gcd(layer_blocks, 7)

    wide_at, m = lax.axis_index("wide"), lax.axis_index("narrow")
    low, me = wide_at // plane, lax.rem(wide_at, plane)
    z = m * Z_LO + low
    core, chip = lax.rem(me, CORES), me // CORES
    twin = me + 1 - 2 * core
    even = lax.rem(low, 2) == 0

    def device(z_at, in_plane):
        return (lax.rem(z_at, Z_LO) * plane + in_plane, z_at // Z_LO)

    def offset(k):
        phase, inner = k // (count // 2), lax.rem(k, count // 2)
        turn, j = lax.rem(inner, 2), inner // 2
        i_x = j // side
        i_y = lax.rem(j, side)

        def far_first(i):
            if side == 1:
                return 0 * i
            return jnp.where(i == 0, 2, jnp.where(i == 1, 1, jnp.where(i == 2, 3, 0)))

        dx, dy = far_first(i_x), far_first(i_y)
        dx = jnp.where(turn == 0, dx, lax.rem(side - dx, side))
        dy = jnp.where(turn == 0, dy, lax.rem(side - dy, side))
        two = jnp.where(even, 2, depth - 2)
        dz = jnp.where(phase == 0, jnp.where(turn == 0, two, 0), jnp.where(turn == 0, 1, depth - 1))
        return dz, dx, dy

    self_k = count // 2 - 1

    def target(k, back=False):
        dz, dx, dy = offset(k)
        if back:
            dz, dx, dy = depth - dz, side - dx, side - dy
        x, y = lax.rem(chip // side + dx, side), lax.rem(lax.rem(chip, side) + dy, side)
        return lax.rem(z + dz, depth), x * side + y

    def partners(body):
        loop(self_k, body)
        loop(count, body, self_k + 1)

    barrier = pltpu.get_barrier_semaphore()

    def greet(where):
        pl.semaphore_signal(barrier, inc=1, device_id=where, device_id_type=MESH)

    def greet_source(k):
        z_at, chip_at = target(k, back=True)
        greet(device(z_at, chip_at * CORES + core))

    def greet_group(k):
        z_at = lax.rem(z + Z_LO * k, depth)
        greet(device(z_at, me))
        greet(device(z_at, twin))

    loop(narrow, greet_group, 1)
    greet(device(z, twin))
    partners(greet_source)

    inputs = [
        (grad_hbm, grad_ref),
        (phi_hbm, phi_ref),
        (weight_hbm, weight_ref),
        (list_hbm, list_ref),
        (local_rows, local_at.at[0:1]),
        (local_cols, local_at.at[1:2]),
        (remote_rows, remote_at.at[0:1]),
        (remote_cols, remote_at.at[1:2]),
        (local_hbm, tiles.at[pl.ds(0, n_local)]),
        (remote_hbm, tiles.at[pl.ds(n_local, n_remote)]),
        (act_hbm, act_ref),
    ]
    inputs = [pltpu.make_async_copy(src, dst, in_sem.at[i]) for i, (src, dst) in enumerate(inputs)]
    for copy in inputs:
        copy.start()

    def make_message(it, adjoint):
        mapped = lax.dot_general(
            adjoint.astype(BF16), weight_ref[...], (((1,), (1,)), ((), ())), preferred_element_type=F32
        )
        message = (mapped * phi_ref[...].astype(F32)).astype(BF16)
        table[it, core, pl.ds(pl.multiple_of(m * rows, rows), rows), :] = message

    for copy in inputs[:3]:
        copy.wait()
    make_message(0, grad_ref[...])
    inputs[3].wait()
    pl.semaphore_wait(barrier, 2 * (narrow - 1) + 1 + count - 1)

    def group_block(it, g, k):
        at = pl.multiple_of(lax.rem(m + narrow - k, narrow) * rows, rows)
        return table.at[it, g, pl.ds(at, rows)]

    def group_copy(it, k):
        return pltpu.make_async_remote_copy(
            src_ref=group_block(it, core, 0),
            dst_ref=group_block(it, core, 0),
            send_sem=group_send.at[it, k],
            recv_sem=group_recv.at[it, k],
            device_id=device(lax.rem(z + Z_LO * k, depth), me),
            device_id_type=MESH,
        )

    def twin_copy(it, k):
        return pltpu.make_async_remote_copy(
            src_ref=group_block(it, core, k),
            dst_ref=group_block(it, core, k),
            send_sem=twin_send.at[it, k],
            recv_sem=twin_recv.at[it, k],
            device_id=device(z, twin),
            device_id_type=MESH,
        )

    away = jnp.where(low < Z_LO // 2, Z_LO - 1, 0)
    stay = jnp.where(low < Z_LO // 2, 0, plane)
    holder = lax.rem(z + jnp.where(low < Z_LO // 2, Z_LO, depth - Z_LO), depth)
    away_rows = pl.ds(pl.multiple_of(away * plane, 8), plane)
    stay_rows = pl.ds(pl.multiple_of(stay, 8), (Z_LO - 1) * plane)

    def list_copies():
        for i, (part_rows, where) in enumerate(
            ((away_rows, device(holder, me)), (away_rows, device(holder, twin)), (stay_rows, device(z, twin)))
        ):
            yield pltpu.make_async_remote_copy(
                src_ref=list_ref.at[part_rows],
                dst_ref=lists.at[core, part_rows],
                send_sem=list_send.at[i],
                recv_sem=list_recv.at[i],
                device_id=where,
                device_id_type=MESH,
            )

    def make_index(g, b):
        turned = jnp.transpose(lists[g, pl.ds(b * plane + core, chips, stride=CORES), :])
        for c in range(chips):
            index[b * chips + c, g * sendn : (g + 1) * sendn, :] = jnp.broadcast_to(turned[:, c : c + 1], (sendn, 128))

    def make_slots():
        def row_of(at, alive, per_row, first):
            key = at[0:1] * per_row + at[1:2]
            slot = lax.broadcasted_iota(jnp.int32, key.shape, 1)
            key = jnp.where(slot < alive, key, -1)
            wide_key = jnp.broadcast_to(key, (128, key.shape[1]))
            pair = lax.broadcasted_iota(jnp.int32, wide_key.shape, 0)
            value = lax.broadcasted_iota(jnp.int32, wide_key.shape, 1) + (first - zero_slot)
            found = zero_slot + jnp.sum(jnp.where(wide_key == pair, value, 0), axis=1, keepdims=True)
            return jnp.transpose(jnp.broadcast_to(found, (128, 128)))[0:1]

        slot_rows[0:1] = row_of(local_at[...], local_count[0], group_blocks, 0)
        slot_rows[1:2] = row_of(remote_at[...], remote_count[0], halo_blocks, n_local)
        copy = pltpu.make_async_copy(slot_rows, slot_of, slot_sem)
        copy.start()
        copy.wait()

    def gather_group(it):
        far_first = sorted(range(1, narrow), key=lambda k: -min(k, narrow - k))
        for k in far_first:
            group_copy(it, k).start()
        twin_copy(it, 0).start()

        @pl.when(it == 0)
        def _():
            for copy in list_copies():
                copy.start()
            lists[core, stay_rows, :] = list_ref[stay_rows, :]
            for copy in inputs[4:8]:
                copy.wait()
            tiles[zero_slot] = jnp.zeros((tb, tb), BF16)
            make_slots()

        for i, k in enumerate(reversed(far_first)):
            group_copy(it, k).wait_recv()
            twin_copy(it, k).start()
            if i == 0:

                @pl.when(it == 0)
                def _():
                    for copy in list_copies():
                        copy.wait()
                    for g in range(CORES):
                        for b in range(Z_LO):
                            make_index(g, b)

        for k in range(narrow):
            twin_copy(it, k).wait_recv()

    my_rows = pl.ds(pl.multiple_of((low * chips + chip) * per_chip, 16), per_chip)

    def swap_copy(it, k):
        z_at, chip_at = target(k)
        return pltpu.make_async_remote_copy(
            src_ref=send.at[it, k],
            dst_ref=halo.at[it, my_rows],
            send_sem=swap_send.at[it, k],
            recv_sem=swap_recv.at[it, k],
            device_id=device(z_at, chip_at * CORES + core),
            device_id_type=MESH,
        )

    def send_batch(it, first):
        wanted = []
        for j in range(batch):
            z_at, chip_at = target(first + j)
            wanted.append(lax.rem(z_at, Z_LO) * chips + chip_at)

        def select(g):
            want = jnp.concatenate([index[w, g * sendn : (g + 1) * sendn, :] for w in wanted], axis=0)
            lane = lax.broadcasted_iota(jnp.int32, want.shape, 1)
            hot = jnp.concatenate(
                [jnp.where(want == lane + at, 1.0, 0.0).astype(BF16) for at in range(0, group_rows, 128)], axis=1
            )
            return jnp.dot(hot, table[it, g], preferred_element_type=F32)

        got = [select(g) for g in range(CORES)]
        for j in range(batch):
            both = jnp.concatenate([rows_of[j * sendn : (j + 1) * sendn] for rows_of in got], axis=0)
            send[it, first + j] = both.astype(BF16)

        def post(j):
            @pl.when(first + j != self_k)
            def _():
                swap_copy(it, first + j).start()

        loop(batch, post)

    def tile_rows(kind, per_row, first, width):
        return jnp.concatenate(
            [
                jnp.concatenate([tiles[slot_of[kind, r * per_row + first + c]] for c in range(width)], axis=1)
                for r in range(blocks)
            ],
            axis=0,
        )

    def layer(it, b):
        def some(i):
            first = b * layer_blocks + i * span
            source = halo[it, pl.ds(pl.multiple_of(first * tb, tb), span * tb), :]
            total[...] += jnp.dot(tile_rows(1, halo_blocks, first, span), source, preferred_element_type=F32)

        loop(layer_blocks // span, some)

    def iterate(it):
        gather_group(it)
        loop(count // batch, lambda c: send_batch(it, c * batch))
        halo[it, my_rows, :] = send[it, self_k]

        @pl.when(it == 0)
        def _():
            for copy in inputs[8:10]:
                copy.wait()

        total[...] = jnp.dot(
            tile_rows(0, group_blocks, 0, group_blocks), table[it, core], preferred_element_type=F32
        )
        arrived = lambda k: swap_copy(it, k).wait_recv()
        loop(self_k, arrived)
        layer(it, low)
        layer(it, lax.rem(low + 2, Z_LO))
        loop(count, arrived, self_k + 1)
        layer(it, lax.rem(low + 1, Z_LO))
        layer(it, lax.rem(low + 3, Z_LO))
        adj_ref[...] = grad_ref[...] + GAMMA * total[...]

        @pl.when(it < ITERS - 1)
        def _():
            make_message(it + 1, adj_ref[...])

    loop(ITERS, iterate)

    inputs[10].wait()
    gradient = lax.dot_general(
        act_ref[...], adj_ref[...].astype(BF16), (((0,), (0,)), ((), ())), preferred_element_type=F32
    )
    piece_rows = hidden // chips
    for j in range(chips):
        part[j] = gradient[j * piece_rows : (j + 1) * piece_rows]

    def share(src, dst, sems, k, where):
        return pltpu.make_async_remote_copy(
            src_ref=src, dst_ref=dst, send_sem=sems[0].at[k], recv_sem=sems[1].at[k], device_id=where, device_id_type=MESH
        )

    def chip_ahead(k):
        return lax.rem(chip + k, chips)

    def plane_copy(k):
        where = device(z, chip_ahead(k) * CORES + core)
        return share(part.at[chip_ahead(k)], plane_sum.at[chip], (plane_send, plane_recv), k, where)

    loop(chips, lambda k: plane_copy(k).start(), 1)
    plane_sum[chip] = part[chip]
    loop(chips, lambda k: plane_copy(k).wait(), 1)

    mine = m * CORES + core
    near_sum[mine] = jnp.sum(plane_sum[...], axis=0)

    def near_copies():
        for k in range(CORES * narrow):
            if k > 0:
                where = device(lax.rem(z + Z_LO * (k // CORES), depth), twin if k % CORES else me)
                yield share(near_sum.at[mine], near_sum.at[mine], (near_send, near_recv), k, where)

    for copy in near_copies():
        copy.start()
    for copy in near_copies():
        copy.wait()

    low_sum[low] = jnp.sum(near_sum[...], axis=0)

    def low_copies():
        for k, step in enumerate((1, depth - 1, jnp.where(even, 2, depth - 2))):
            where = device(lax.rem(z + step, depth), me)
            yield share(low_sum.at[low], low_sum.at[low], (low_send, low_recv), k, where)

    for copy in low_copies():
        copy.start()
    for copy in low_copies():
        copy.wait()
    wg_all[chip] = jnp.sum(low_sum[...], axis=0) * scale

    def last_copy(k):
        where = device(z, chip_ahead(k) * CORES + core)
        return share(wg_all.at[chip], wg_all.at[chip], (last_send, last_recv), k, where)

    loop(chips, lambda k: last_copy(k).start(), 1)
    loop(chips, lambda k: last_copy(k).wait(), 1)
    wg_ref[...] = wg_all[...]

    def sent(it):
        for k in range(1, narrow):
            group_copy(it, k).wait_send()
        for k in range(narrow):
            twin_copy(it, k).wait_send()
        partners(lambda k: swap_copy(it, k).wait_send())

    loop(ITERS, sent)


def per_device(
    grad_in,
    phi_slope,
    activations,
    weight,
    local_tiles,
    local_rows,
    local_cols,
    local_count,
    remote_tiles,
    remote_rows,
    remote_cols,
    remote_count,
    send_list,
):
    wide, narrow = lax.axis_size("wide"), lax.axis_size("narrow")
    plane = wide // Z_LO
    chips = plane // CORES
    rows, hidden = grad_in.shape
    tb = local_tiles.shape[2]
    sendn = send_list.shape[2]
    n_local, n_remote = local_tiles.shape[1], remote_tiles.shape[1]
    count = Z_LO * chips
    batch = math.gcd(count // 2, 8)
    scale = GAMMA / math.sqrt(rows * wide * narrow)
    vmem = pl.BlockSpec(memory_space=pltpu.VMEM)
    hbm = pl.BlockSpec(memory_space=pltpu.HBM)
    smem = pl.BlockSpec(memory_space=pltpu.SMEM)
    piece = (hidden // chips, hidden)
    dma = pltpu.SemaphoreType.DMA
    pair = lambda *shape: [dma(shape), dma(shape)]
    adjoint, weight_grad = pl.pallas_call(
        functools.partial(kernel, (plane, narrow, rows, tb, sendn, batch, scale)),
        out_shape=(
            jax.ShapeDtypeStruct((rows, hidden), F32),
            jax.ShapeDtypeStruct((chips,) + piece, F32),
        ),
        in_specs=[smem] * 2 + [hbm] * 11,
        out_specs=(vmem, vmem),
        scratch_shapes=[
            pltpu.VMEM((rows, hidden), F32),
            pltpu.VMEM((rows, hidden), BF16),
            pltpu.VMEM((rows, hidden), BF16),
            pltpu.VMEM((hidden, hidden), BF16),
            pltpu.VMEM((wide, sendn), jnp.int32),
            pltpu.VMEM((n_local + n_remote + 1, tb, tb), BF16),
            pltpu.VMEM((2, n_local), jnp.int32),
            pltpu.VMEM((2, n_remote), jnp.int32),
            pltpu.VMEM((8, 128), jnp.int32),
            pltpu.SMEM((8, 128), jnp.int32),
            pltpu.VMEM((ITERS, CORES, narrow * rows, hidden), BF16),
            pltpu.VMEM((CORES, wide, sendn), jnp.int32),
            pltpu.VMEM((count, CORES * sendn, 128), jnp.int32),
            pltpu.VMEM((ITERS, count, CORES * sendn, hidden), BF16),
            pltpu.VMEM((ITERS, wide * sendn, hidden), BF16),
            pltpu.VMEM((rows, hidden), F32),
            pltpu.VMEM((chips,) + piece, F32),
            pltpu.VMEM((chips,) + piece, F32),
            pltpu.VMEM((CORES * narrow,) + piece, F32),
            pltpu.VMEM((Z_LO,) + piece, F32),
            pltpu.VMEM((chips,) + piece, F32),
            dma((11,)),
            dma,
        ]
        + pair(3)
        + pair(ITERS, narrow)
        + pair(ITERS, narrow)
        + pair(ITERS, count)
        + pair(chips)
        + pair(CORES * narrow)
        + pair(3)
        + pair(chips),
        compiler_params=pltpu.CompilerParams(
            collective_id=0, has_side_effects=True, vmem_limit_bytes=61 * 1024 * 1024
        ),
    )(
        local_count,
        remote_count,
        grad_in,
        phi_slope,
        activations,
        weight,
        send_list[0],
        local_tiles[0],
        remote_tiles[0],
        local_rows,
        local_cols,
        remote_rows,
        remote_cols,
    )
    return adjoint, weight_grad.reshape(hidden, hidden)


def solution(mesh):
    placed = (
        P(("wide", "narrow"), None),
        P(("wide", "narrow"), None),
        P(("wide", "narrow"), None),
        P(),
        P(("wide", "narrow"), None, None, None),
        P(("wide", "narrow"), None),
        P(("wide", "narrow"), None),
        P(("wide", "narrow")),
        P(("wide", "narrow"), None, None, None),
        P(("wide", "narrow"), None),
        P(("wide", "narrow"), None),
        P(("wide", "narrow")),
        P(("wide", "narrow"), None, None),
    )
    return jax.shard_map(
        per_device,
        mesh=mesh,
        in_specs=placed,
        out_specs=(P(("wide", "narrow"), None), P()),
        check_vma=False,
    )
```

time: 688 us -> 143 us (0.21)
  waiting for transfers between devices: 478 us -> 0 us
  Pallas kernels: 0 us -> 136 us
  blocking collectives: 97.1 us -> 0 us
  local copies, waits for them, and re-layouts: 54.7 us -> 4.52 us
  matrix products: 25.1 us -> 0 us
  between operations: 15.6 us -> 1.93 us
  starting transfers between devices: 13.4 us -> 0 us
    psum x1 -> x0, waiting for transfers between devices: 433 us -> none  [per_device(): summed = lax.psum(partial_sum, ('wide', 'narrow'))]
    pallas_call x0 -> x1, Pallas kernels: none -> 136 us  [per_device(): pl.pallas_call(functools.partial(kernel, (plane, narrow, rows, tb, sendn,...]
    all_to_all x1 -> x0, blocking collectives: 53.6 us -> none  [per_device(): lax.all_to_all(outgoing, 'wide', split_axis=0, concat_axis=0, tiled=True)]
    gather x4 -> x0, local copies, waits for them, and re-layouts: 52.5 us -> none  [the longest x2 46.6 us: per_device(): outgoing = gathered[send_list[0]]]
    all_to_all x1 -> x0, waiting for transfers between devices: 44.7 us -> none  [per_device(): lax.all_to_all(outgoing, 'wide', split_axis=0, concat_axis=0, tiled=True)]
    all_gather x2 -> x0, blocking collectives: 43.5 us -> none  [per_device(): gathered = lax.all_gather(message, 'narrow', axis=0, tiled=True)]
    dot_general x7 -> x0, matrix products: 25.1 us -> none  [the longest x2 14.1 us: tile_product(): jnp.einsum('rk,kih->rih', table, product, precision=lax.Precision.HIGHEST)]
    all_to_all x1 -> x0, starting transfers between devices: 13.1 us -> none  [per_device(): lax.all_to_all(outgoing, 'wide', split_axis=0, concat_axis=0, tiled=True)]
  transfers between devices with their start and end apart: 2 -> 0, of which waited for: 2 -> 0; matrix products, arithmetic and copies ran while one was open for 0% -> 0% of each run, Pallas kernels for 0% -> 0%
where the time goes in v2:
time: 143 us; the launch traced here: 142 us
  Pallas kernels  136 us (95%)
  local copies, waits for them, and re-layouts  4.52 us (3%)
  between operations  1.93 us (1%)
    pallas_call x1, Pallas kernels, per_device(): pl.pallas_call(functools.partial(kernel, (plane, narrow, rows, tb, sendn,...  136 us
    unnamed x3, local copies, waits for them, and re-layouts  4.52 us

profile of v2, /device:TPU:1, one launch (start us, length us, event | category | flops | bytes accessed | tf_op | source)
XLA Modules:
  0.0 142.4 jit_solution(12522701219777982965)
XLA Ops:
  1.9 1.5 %copy.15 = s32[1,128,56]{2,1,0:T(8,128)} copy(s32[1,128,56]{1,2,0:T(8,128)} %param.25) | data formatting | bytes 57344 | tf_op args[12]
  3.4 135.9 %shard_map.140 = (f32[256,128]{1,0:T(8,128)}, f32[16,8,128]{2,1,0:T(8,128)}) custom-call(s32[1]{0:T(128)S(6)} %copy.18.local_count, s32[1]{0:T(128)S(6)} %copy.19.remote_count, f32[256,128]{1,0:T(8,128)} %grad_hbm.1, bf16[256,128]{1,0:T(8,128)(2,1)} %phi_hbm.1, bf16[256,128]{1,0:T(8,128)(2,1)} %act_hbm.1, bf16[128,128]{1,0:T(8,128)(2,1)} %weight_hbm.1, ...), custom_call_target="tpu_custom_call" | custom-call | tf_op jit(solution)/shard_map/pallas_call | solution.py:471
  139.3 1.6 %copy.20 = f32[256,128]{1,0:T(8,128)} copy(f32[256,128]{1,0:T(8,128)} %get-tuple-element.8) | data formatting | bytes 262144
  140.9 1.5 %copy.21 = f32[128,128]{1,0:T(8,128)} copy(f32[128,128]{1,0:T(8,128)} %bitcast.7) | data formatting | bytes 131072

commit v3 on v2

--- a/solution.py
+++ b/solution.py
@@ -40,8 +40,9 @@
     local_cols,
     remote_rows,
     remote_cols,
+    adj_hbm,
+    wg_ref,
     adj_ref,
-    wg_ref,
     grad_ref,
     phi_ref,
     act_ref,
@@ -55,16 +56,19 @@
     table,
     lists,
     index,
+    picked,
     send,
     halo,
     total,
     part,
     plane_sum,
-    near_sum,
-    low_sum,
+    column_sum,
     wg_all,
+    know_plane,
+    know_space,
     in_sem,
     slot_sem,
+    out_sem,
     list_send,
     list_recv,
     group_send,
@@ -75,10 +79,8 @@
     swap_recv,
     plane_send,
     plane_recv,
-    near_send,
-    near_recv,
-    low_send,
-    low_recv,
+    column_send,
+    column_recv,
     last_send,
     last_recv,
 ):
@@ -128,12 +130,9 @@
 
     self_k = count // 2 - 1
 
-    def target(k, back=False):
+    def target(k):
         dz, dx, dy = offset(k)
-        if back:
-            dz, dx, dy = depth - dz, side - dx, side - dy
-        x, y = lax.rem(chip // side + dx, side), lax.rem(lax.rem(chip, side) + dy, side)
-        return lax.rem(z + dz, depth), x * side + y
+        return lax.rem(z + dz, depth), lax.rem(chip // side + dx, side) * side + lax.rem(lax.rem(chip, side) + dy, side)
 
     def partners(body):
         loop(self_k, body)
@@ -144,18 +143,20 @@
     def greet(where):
         pl.semaphore_signal(barrier, inc=1, device_id=where, device_id_type=MESH)
 
-    def greet_source(k):
-        z_at, chip_at = target(k, back=True)
-        greet(device(z_at, chip_at * CORES + core))
-
-    def greet_group(k):
-        z_at = lax.rem(z + Z_LO * k, depth)
-        greet(device(z_at, me))
-        greet(device(z_at, twin))
-
-    loop(narrow, greet_group, 1)
-    greet(device(z, twin))
-    partners(greet_source)
+    x, y = chip // side, lax.rem(chip, side)
+    x_line = [device(z, (lax.rem(x + k, side) * side + y) * CORES + core) for k in range(1, side)]
+    y_line = [device(z, (x * side + lax.rem(y + k, side)) * CORES + core) for k in range(1, side)]
+    z_line = [device(lax.rem(z + k, depth), me) for k in (1, 2, depth - 2, depth - 1)]
+    group = [device(lax.rem(z + Z_LO * k, depth), me) for k in range(1, narrow)]
+    first_round = z_line + group + x_line + y_line + [device(z, twin)]
+    for where in first_round:
+        greet(where)
+
+    def tell(semaphore, listeners):
+        for where in listeners:
+            pl.semaphore_signal(semaphore, inc=1, device_id=where, device_id_type=MESH)
+        if listeners:
+            pl.semaphore_wait(semaphore, len(listeners))
 
     inputs = [
         (grad_hbm, grad_ref),
@@ -184,8 +185,7 @@
     for copy in inputs[:3]:
         copy.wait()
     make_message(0, grad_ref[...])
-    inputs[3].wait()
-    pl.semaphore_wait(barrier, 2 * (narrow - 1) + 1 + count - 1)
+    pl.semaphore_wait(barrier, len(first_round))
 
     def group_block(it, g, k):
         at = pl.multiple_of(lax.rem(m + narrow - k, narrow) * rows, rows)
@@ -212,28 +212,31 @@
         )
 
     away = jnp.where(low < Z_LO // 2, Z_LO - 1, 0)
-    stay = jnp.where(low < Z_LO // 2, 0, plane)
     holder = lax.rem(z + jnp.where(low < Z_LO // 2, Z_LO, depth - Z_LO), depth)
-    away_rows = pl.ds(pl.multiple_of(away * plane, 8), plane)
-    stay_rows = pl.ds(pl.multiple_of(stay, 8), (Z_LO - 1) * plane)
-
-    def list_copies():
-        for i, (part_rows, where) in enumerate(
-            ((away_rows, device(holder, me)), (away_rows, device(holder, twin)), (stay_rows, device(z, twin)))
-        ):
-            yield pltpu.make_async_remote_copy(
-                src_ref=list_ref.at[part_rows],
-                dst_ref=lists.at[core, part_rows],
-                send_sem=list_send.at[i],
-                recv_sem=list_recv.at[i],
-                device_id=where,
-                device_id_type=MESH,
-            )
-
-    def make_index(g, b):
-        turned = jnp.transpose(lists[g, pl.ds(b * plane + core, chips, stride=CORES), :])
-        for c in range(chips):
-            index[b * chips + c, g * sendn : (g + 1) * sendn, :] = jnp.broadcast_to(turned[:, c : c + 1], (sendn, 128))
+
+    def list_copy(i):
+        src, kind, where = (
+            (list_ref, 1, device(holder, me)),
+            (list_ref, 0, device(z, twin)),
+            (lists.at[1, core], 1, device(z, twin)),
+        )[i]
+        return pltpu.make_async_remote_copy(
+            src_ref=src,
+            dst_ref=lists.at[kind, core],
+            send_sem=list_send.at[i],
+            recv_sem=list_recv.at[i],
+            device_id=where,
+            device_id_type=MESH,
+        )
+
+    def make_index(g):
+        lane = lax.broadcasted_iota(jnp.int32, (sendn, Z_LO * plane), 1)
+        is_away = (lane >= away * plane) & (lane < (away + 1) * plane)
+        merged = jnp.where(is_away, lists[1, g], lists[0, g])
+        merged = jnp.where(core == 0, merged, pltpu.roll(merged, Z_LO * plane - 1, 1))
+        for c in range(count):
+            at = c * CORES
+            index[c, g * sendn : (g + 1) * sendn, :] = jnp.broadcast_to(merged[:, at : at + 1], (sendn, 128))
 
     def make_slots():
         def row_of(at, alive, per_row, first):
@@ -252,38 +255,6 @@
         copy.start()
         copy.wait()
 
-    def gather_group(it):
-        far_first = sorted(range(1, narrow), key=lambda k: -min(k, narrow - k))
-        for k in far_first:
-            group_copy(it, k).start()
-        twin_copy(it, 0).start()
-
-        @pl.when(it == 0)
-        def _():
-            for copy in list_copies():
-                copy.start()
-            lists[core, stay_rows, :] = list_ref[stay_rows, :]
-            for copy in inputs[4:8]:
-                copy.wait()
-            tiles[zero_slot] = jnp.zeros((tb, tb), BF16)
-            make_slots()
-
-        for i, k in enumerate(reversed(far_first)):
-            group_copy(it, k).wait_recv()
-            twin_copy(it, k).start()
-            if i == 0:
-
-                @pl.when(it == 0)
-                def _():
-                    for copy in list_copies():
-                        copy.wait()
-                    for g in range(CORES):
-                        for b in range(Z_LO):
-                            make_index(g, b)
-
-        for k in range(narrow):
-            twin_copy(it, k).wait_recv()
-
     my_rows = pl.ds(pl.multiple_of((low * chips + chip) * per_chip, 16), per_chip)
 
     def swap_copy(it, k):
@@ -297,31 +268,39 @@
             device_id_type=MESH,
         )
 
-    def send_batch(it, first):
+    batches = count // batch
+    early = batches // 2
+
+    def select(it, c, g):
         wanted = []
         for j in range(batch):
-            z_at, chip_at = target(first + j)
+            z_at, chip_at = target(c * batch + j)
             wanted.append(lax.rem(z_at, Z_LO) * chips + chip_at)
-
-        def select(g):
-            want = jnp.concatenate([index[w, g * sendn : (g + 1) * sendn, :] for w in wanted], axis=0)
-            lane = lax.broadcasted_iota(jnp.int32, want.shape, 1)
-            hot = jnp.concatenate(
-                [jnp.where(want == lane + at, 1.0, 0.0).astype(BF16) for at in range(0, group_rows, 128)], axis=1
-            )
-            return jnp.dot(hot, table[it, g], preferred_element_type=F32)
-
-        got = [select(g) for g in range(CORES)]
+        g_rows = pl.ds(pl.multiple_of(g * sendn, 8), sendn)
+        want = jnp.concatenate([index[w, g_rows, :] for w in wanted], axis=0)
+        lane = lax.broadcasted_iota(jnp.int32, want.shape, 1)
+        hot = jnp.concatenate(
+            [jnp.where(want == lane + at, 1.0, 0.0).astype(BF16) for at in range(0, group_rows, 128)], axis=1
+        )
+        got = jnp.dot(hot, table[it, g], preferred_element_type=F32)
         for j in range(batch):
-            both = jnp.concatenate([rows_of[j * sendn : (j + 1) * sendn] for rows_of in got], axis=0)
-            send[it, first + j] = both.astype(BF16)
-
+            picked[c, j, g_rows, :] = got[j * sendn : (j + 1) * sendn]
+
+    def send_batch(it, c):
         def post(j):
-            @pl.when(first + j != self_k)
+            k = c * batch + j
+            send[it, k] = picked[c, j].astype(BF16)
+
+            @pl.when(k != self_k)
             def _():
-                swap_copy(it, first + j).start()
-
+                swap_copy(it, k).start()
+
+        select(it, c, 1 - core)
         loop(batch, post)
+
+    def both_then_send(it, c):
+        select(it, c, core)
+        send_batch(it, c)
 
     def tile_rows(kind, per_row, first, width):
         return jnp.concatenate(
@@ -332,6 +311,50 @@
             axis=0,
         )
 
+    def gather_group(it):
+        far_first = sorted(range(1, narrow), key=lambda k: -min(k, narrow - k))
+        for k in far_first:
+            group_copy(it, k).start()
+        twin_copy(it, 0).start()
+
+        @pl.when(it == 0)
+        def _():
+            inputs[3].wait()
+            list_copy(0).start()
+            list_copy(1).start()
+            lists[0, core] = list_ref[...]
+            tell(know_plane, x_line)
+            tell(know_space, z_line + [device(z, twin)])
+            for copy in inputs[4:8]:
+                copy.wait()
+            tiles[zero_slot] = jnp.zeros((tb, tb), BF16)
+            make_slots()
+
+        for i, k in enumerate(reversed(far_first)):
+            group_copy(it, k).wait_recv()
+            twin_copy(it, k).start()
+            if i == 0:
+
+                @pl.when(it == 0)
+                def _():
+                    list_copy(0).wait_recv()
+                    list_copy(2).start()
+                    list_copy(1).wait_recv()
+                    list_copy(2).wait_recv()
+                    for g in range(CORES):
+                        make_index(g)
+                    for i in range(3):
+                        list_copy(i).wait_send()
+                    for copy in inputs[8:10]:
+                        copy.wait()
+
+        loop(early, lambda c: select(it, c, core))
+        total[...] = jnp.dot(
+            tile_rows(0, group_blocks, 0, group_blocks), table[it, core], preferred_element_type=F32
+        )
+        for k in range(narrow):
+            twin_copy(it, k).wait_recv()
+
     def layer(it, b):
         def some(i):
             first = b * layer_blocks + i * span
@@ -342,17 +365,9 @@
 
     def iterate(it):
         gather_group(it)
-        loop(count // batch, lambda c: send_batch(it, c * batch))
+        loop(early, lambda c: send_batch(it, c))
+        loop(batches, lambda c: both_then_send(it, c), early)
         halo[it, my_rows, :] = send[it, self_k]
-
-        @pl.when(it == 0)
-        def _():
-            for copy in inputs[8:10]:
-                copy.wait()
-
-        total[...] = jnp.dot(
-            tile_rows(0, group_blocks, 0, group_blocks), table[it, core], preferred_element_type=F32
-        )
         arrived = lambda k: swap_copy(it, k).wait_recv()
         loop(self_k, arrived)
         layer(it, low)
@@ -367,6 +382,8 @@
             make_message(it + 1, adj_ref[...])
 
     loop(ITERS, iterate)
+    adj_copy = pltpu.make_async_copy(adj_ref, adj_hbm, out_sem)
+    adj_copy.start()
 
     inputs[10].wait()
     gradient = lax.dot_general(
@@ -385,47 +402,34 @@
         return lax.rem(chip + k, chips)
 
     def plane_copy(k):
-        where = device(z, chip_ahead(k) * CORES + core)
-        return share(part.at[chip_ahead(k)], plane_sum.at[chip], (plane_send, plane_recv), k, where)
-
-    loop(chips, lambda k: plane_copy(k).start(), 1)
-    plane_sum[chip] = part[chip]
-    loop(chips, lambda k: plane_copy(k).wait(), 1)
-
-    mine = m * CORES + core
-    near_sum[mine] = jnp.sum(plane_sum[...], axis=0)
-
-    def near_copies():
-        for k in range(CORES * narrow):
-            if k > 0:
-                where = device(lax.rem(z + Z_LO * (k // CORES), depth), twin if k % CORES else me)
-                yield share(near_sum.at[mine], near_sum.at[mine], (near_send, near_recv), k, where)
-
-    for copy in near_copies():
-        copy.start()
-    for copy in near_copies():
-        copy.wait()
-
-    low_sum[low] = jnp.sum(near_sum[...], axis=0)
-
-    def low_copies():
-        for k, step in enumerate((1, depth - 1, jnp.where(even, 2, depth - 2))):
-            where = device(lax.rem(z + step, depth), me)
-            yield share(low_sum.at[low], low_sum.at[low], (low_send, low_recv), k, where)
-
-    for copy in low_copies():
-        copy.start()
-    for copy in low_copies():
-        copy.wait()
-    wg_all[chip] = jnp.sum(low_sum[...], axis=0) * scale
+        other = lax.rem(me + k, plane)
+        return share(part.at[other // CORES], plane_sum.at[me], (plane_send, plane_recv), k, device(z, other))
+
+    loop(plane, lambda k: plane_copy(k).start(), 1)
+    plane_sum[me] = part[chip]
+    loop(plane, lambda k: plane_copy(k).wait_recv(), 1)
+    column_sum[z] = jnp.sum(plane_sum[...], axis=0)
+
+    def column_copy(k):
+        where = device(lax.rem(z + k, depth), me)
+        return share(column_sum.at[z], column_sum.at[z], (column_send, column_recv), k, where)
+
+    for k in sorted(range(1, depth), key=lambda k: -min(k, depth - k)):
+        column_copy(k).start()
+    loop(depth, lambda k: column_copy(k).wait_recv(), 1)
+    wg_all[chip] = jnp.sum(column_sum[...], axis=0) * scale
 
     def last_copy(k):
         where = device(z, chip_ahead(k) * CORES + core)
         return share(wg_all.at[chip], wg_all.at[chip], (last_send, last_recv), k, where)
 
     loop(chips, lambda k: last_copy(k).start(), 1)
-    loop(chips, lambda k: last_copy(k).wait(), 1)
+    loop(chips, lambda k: last_copy(k).wait_recv(), 1)
     wg_ref[...] = wg_all[...]
+    loop(plane, lambda k: plane_copy(k).wait_send(), 1)
+    loop(depth, lambda k: column_copy(k).wait_send(), 1)
+    loop(chips, lambda k: last_copy(k).wait_send(), 1)
+    adj_copy.wait()
 
     def sent(it):
         for k in range(1, narrow):
@@ -475,39 +479,42 @@
             jax.ShapeDtypeStruct((chips,) + piece, F32),
         ),
         in_specs=[smem] * 2 + [hbm] * 11,
-        out_specs=(vmem, vmem),
+        out_specs=(hbm, vmem),
         scratch_shapes=[
+            pltpu.VMEM((rows, hidden), F32),
             pltpu.VMEM((rows, hidden), F32),
             pltpu.VMEM((rows, hidden), BF16),
             pltpu.VMEM((rows, hidden), BF16),
             pltpu.VMEM((hidden, hidden), BF16),
-            pltpu.VMEM((wide, sendn), jnp.int32),
+            pltpu.VMEM((sendn, wide), jnp.int32),
             pltpu.VMEM((n_local + n_remote + 1, tb, tb), BF16),
             pltpu.VMEM((2, n_local), jnp.int32),
             pltpu.VMEM((2, n_remote), jnp.int32),
             pltpu.VMEM((8, 128), jnp.int32),
             pltpu.SMEM((8, 128), jnp.int32),
             pltpu.VMEM((ITERS, CORES, narrow * rows, hidden), BF16),
-            pltpu.VMEM((CORES, wide, sendn), jnp.int32),
+            pltpu.VMEM((2, CORES, sendn, wide), jnp.int32),
             pltpu.VMEM((count, CORES * sendn, 128), jnp.int32),
+            pltpu.VMEM((count // batch, batch, CORES * sendn, hidden), F32),
             pltpu.VMEM((ITERS, count, CORES * sendn, hidden), BF16),
             pltpu.VMEM((ITERS, wide * sendn, hidden), BF16),
             pltpu.VMEM((rows, hidden), F32),
             pltpu.VMEM((chips,) + piece, F32),
+            pltpu.VMEM((plane,) + piece, F32),
+            pltpu.VMEM((Z_LO * narrow,) + piece, F32),
             pltpu.VMEM((chips,) + piece, F32),
-            pltpu.VMEM((CORES * narrow,) + piece, F32),
-            pltpu.VMEM((Z_LO,) + piece, F32),
-            pltpu.VMEM((chips,) + piece, F32),
+            pltpu.SemaphoreType.REGULAR,
+            pltpu.SemaphoreType.REGULAR,
             dma((11,)),
+            dma,
             dma,
         ]
         + pair(3)
         + pair(ITERS, narrow)
         + pair(ITERS, narrow)
         + pair(ITERS, count)
-        + pair(chips)
-        + pair(CORES * narrow)
-        + pair(3)
+        + pair(plane)
+        + pair(Z_LO * narrow)
         + pair(chips),
         compiler_params=pltpu.CompilerParams(
             collective_id=0, has_side_effects=True, vmem_limit_bytes=61 * 1024 * 1024
@@ -519,7 +526,7 @@
         phi_slope,
         activations,
         weight,
-        send_list[0],
+        jnp.transpose(send_list[0]),
         local_tiles[0],
         remote_tiles[0],
         local_rows,

time: 143 us -> 135 us (0.944)
  Pallas kernels: 136 us -> 130 us
  local copies, waits for them, and re-layouts: 4.52 us -> 3.04 us
    pallas_call x1, Pallas kernels: 136 us -> 130 us  [per_device(): pl.pallas_call(functools.partial(kernel, (plane, narrow, rows, tb, sendn,...]
    unnamed x3 -> x2, local copies, waits for them, and re-layouts: 4.52 us -> 3.04 us
where the time goes in v3:
time: 135 us
  Pallas kernels  130 us (96%)
  local copies, waits for them, and re-layouts  3.04 us (2%)
  between operations  1.93 us (1%)
    pallas_call x1, Pallas kernels, per_device(): pl.pallas_call(functools.partial(kernel, (plane, narrow, rows, tb, sendn,...  130 us
    unnamed x2, local copies, waits for them, and re-layouts  3.04 us

profile of v3, /device:TPU:1, one launch (start us, length us, event | category | flops | bytes accessed | tf_op | source)
XLA Modules:
  0.0 134.5 jit_solution(3433017141100826371)
XLA Ops:
  1.9 129.6 %shard_map.140 = (f32[256,128]{1,0:T(8,128)}, f32[16,8,128]{2,1,0:T(8,128)}) custom-call(s32[1]{0:T(128)S(6)} %copy.17.local_count, s32[1]{0:T(128)S(6)} %copy.18.remote_count, f32[256,128]{1,0:T(8,128)} %grad_hbm.1, bf16[256,128]{1,0:T(8,128)(2,1)} %phi_hbm.1, bf16[256,128]{1,0:T(8,128)(2,1)} %act_hbm.1, bf16[128,128]{1,0:T(8,128)(2,1)} %weight_hbm.1, ...), custom_call_target="tpu_custom_call" | custom-call | tf_op jit(solution)/shard_map/pallas_call | solution.py:475
  131.5 1.6 %copy.19 = f32[256,128]{1,0:T(8,128)} copy(f32[256,128]{1,0:T(8,128)} %get-tuple-element.8) | data formatting | bytes 262144
  133.1 1.5 %copy.20 = f32[128,128]{1,0:T(8,128)} copy(f32[128,128]{1,0:T(8,128)} %bitcast.8) | data formatting | bytes 131072

commit v4 on v3

--- a/solution.py
+++ b/solution.py
@@ -122,6 +122,7 @@
             return jnp.where(i == 0, 2, jnp.where(i == 1, 1, jnp.where(i == 2, 3, 0)))
 
         dx, dy = far_first(i_x), far_first(i_y)
+        dx, dy = jnp.where(core == 0, dx, dy), jnp.where(core == 0, dy, dx)
         dx = jnp.where(turn == 0, dx, lax.rem(side - dx, side))
         dy = jnp.where(turn == 0, dy, lax.rem(side - dy, side))
         two = jnp.where(even, 2, depth - 2)
@@ -187,26 +188,33 @@
     make_message(0, grad_ref[...])
     pl.semaphore_wait(barrier, len(first_round))
 
-    def group_block(it, g, k):
-        at = pl.multiple_of(lax.rem(m + narrow - k, narrow) * rows, rows)
-        return table.at[it, g, pl.ds(at, rows)]
-
-    def group_copy(it, k):
+    half = rows // 2
+
+    def group_half(it, k, piece):
+        at = pl.multiple_of(lax.rem(m + narrow - k, narrow) * rows + piece * half, half)
+        return table.at[it, core, pl.ds(at, half)]
+
+    hops = ((1, 0, 0), (-1, 0, 1), (1, 0, 1), (-1, 0, 0), (1, 1, 0), (-1, narrow - 1, 1))
+
+    def group_copy(it, i):
+        way, k, piece = hops[i]
+        ref = group_half(it, k, piece)
         return pltpu.make_async_remote_copy(
-            src_ref=group_block(it, core, 0),
-            dst_ref=group_block(it, core, 0),
-            send_sem=group_send.at[it, k],
-            recv_sem=group_recv.at[it, k],
-            device_id=device(lax.rem(z + Z_LO * k, depth), me),
+            src_ref=ref,
+            dst_ref=ref,
+            send_sem=group_send.at[it, i],
+            recv_sem=group_recv.at[it, i],
+            device_id=device(lax.rem(z + depth + way * Z_LO, depth), me),
             device_id_type=MESH,
         )
 
-    def twin_copy(it, k):
+    def twin_copy(it, k, piece):
+        ref = group_half(it, k, piece)
         return pltpu.make_async_remote_copy(
-            src_ref=group_block(it, core, k),
-            dst_ref=group_block(it, core, k),
-            send_sem=twin_send.at[it, k],
-            recv_sem=twin_recv.at[it, k],
+            src_ref=ref,
+            dst_ref=ref,
+            send_sem=twin_send.at[it, CORES * k + piece],
+            recv_sem=twin_recv.at[it, CORES * k + piece],
             device_id=device(z, twin),
             device_id_type=MESH,
         )
@@ -312,10 +320,10 @@
         )
 
     def gather_group(it):
-        far_first = sorted(range(1, narrow), key=lambda k: -min(k, narrow - k))
-        for k in far_first:
-            group_copy(it, k).start()
-        twin_copy(it, 0).start()
+        for i in range(4):
+            group_copy(it, i).start()
+        for piece in range(2):
+            twin_copy(it, 0, piece).start()
 
         @pl.when(it == 0)
         def _():
@@ -325,35 +333,40 @@
             lists[0, core] = list_ref[...]
             tell(know_plane, x_line)
             tell(know_space, z_line + [device(z, twin)])
+
+        for i in range(2):
+            group_copy(it, i).wait_recv()
+            group_copy(it, i + 4).start()
+
+        @pl.when(it == 0)
+        def _():
             for copy in inputs[4:8]:
                 copy.wait()
             tiles[zero_slot] = jnp.zeros((tb, tb), BF16)
             make_slots()
-
-        for i, k in enumerate(reversed(far_first)):
-            group_copy(it, k).wait_recv()
-            twin_copy(it, k).start()
-            if i == 0:
-
-                @pl.when(it == 0)
-                def _():
-                    list_copy(0).wait_recv()
-                    list_copy(2).start()
-                    list_copy(1).wait_recv()
-                    list_copy(2).wait_recv()
-                    for g in range(CORES):
-                        make_index(g)
-                    for i in range(3):
-                        list_copy(i).wait_send()
-                    for copy in inputs[8:10]:
-                        copy.wait()
+            list_copy(0).wait_recv()
+            list_copy(2).start()
+            list_copy(1).wait_recv()
+            list_copy(2).wait_recv()
+            for g in range(CORES):
+                make_index(g)
+            for i in range(3):
+                list_copy(i).wait_send()
+            for copy in inputs[8:10]:
+                copy.wait()
+
+        for i, (way, k, piece) in enumerate(hops):
+            if i > 1:
+                group_copy(it, i).wait_recv()
+            twin_copy(it, (k + narrow + way) % narrow, piece).start()
 
         loop(early, lambda c: select(it, c, core))
         total[...] = jnp.dot(
             tile_rows(0, group_blocks, 0, group_blocks), table[it, core], preferred_element_type=F32
         )
         for k in range(narrow):
-            twin_copy(it, k).wait_recv()
+            for piece in range(2):
+                twin_copy(it, k, piece).wait_recv()
 
     def layer(it, b):
         def some(i):
@@ -432,13 +445,25 @@
     adj_copy.wait()
 
     def sent(it):
-        for k in range(1, narrow):
-            group_copy(it, k).wait_send()
+        for i in range(len(hops)):
+            group_copy(it, i).wait_send()
         for k in range(narrow):
-            twin_copy(it, k).wait_send()
+            for piece in range(2):
+                twin_copy(it, k, piece).wait_send()
         partners(lambda k: swap_copy(it, k).wait_send())
 
     loop(ITERS, sent)
+
+
+def hand_on(adj_src, wg_src, adj_dst, wg_dst, sems):
+    copies = [
+        pltpu.make_async_copy(adj_src, adj_dst, sems.at[0]),
+        pltpu.make_async_copy(wg_src, wg_dst, sems.at[1]),
+    ]
+    for copy in copies:
+        copy.start()
+    for copy in copies:
+        copy.wait()
 
 
 def per_device(
@@ -510,8 +535,8 @@
             dma,
         ]
         + pair(3)
-        + pair(ITERS, narrow)
-        + pair(ITERS, narrow)
+        + pair(ITERS, 6)
+        + pair(ITERS, CORES * narrow)
         + pair(ITERS, count)
         + pair(plane)
         + pair(Z_LO * narrow)
@@ -534,7 +559,16 @@
         remote_rows,
         remote_cols,
     )
-    return adjoint, weight_grad.reshape(hidden, hidden)
+    return pl.pallas_call(
+        hand_on,
+        out_shape=(
+            jax.ShapeDtypeStruct((rows, hidden), F32),
+            jax.ShapeDtypeStruct((hidden, hidden), F32),
+        ),
+        in_specs=[vmem] * 2,
+        out_specs=(hbm, hbm),
+        scratch_shapes=[dma((2,))],
+    )(adjoint, weight_grad.reshape(hidden, hidden))
 
 
 def solution(mesh):

time: 135 us -> 126 us (0.933)
  Pallas kernels: 130 us -> 124 us
  local copies, waits for them, and re-layouts: 3.04 us -> 0 us
    pallas_call x1, Pallas kernels: 130 us -> 122 us  [per_device(): pl.pallas_call(functools.partial(kernel, (plane, narrow, rows, tb, sendn,...]
    unnamed x2 -> x0, local copies, waits for them, and re-layouts: 3.04 us -> none
    pallas_call x0 -> x1, Pallas kernels: none -> 1.6 us  [per_device(): pl.pallas_call(hand_on, out_shape=(jax.ShapeDtypeStruct((rows, hidden), F...]
where the time goes in v4:
time: 126 us
  Pallas kernels  124 us (98%)
  between operations  1.93 us (2%)
    pallas_call x1, Pallas kernels, per_device(): pl.pallas_call(functools.partial(kernel, (plane, narrow, rows, tb, sendn,...  122 us

profile of v4, /device:TPU:1, one launch (start us, length us, event | category | flops | bytes accessed | tf_op | source)
XLA Modules:
  0.0 125.8 jit_solution(7764754348959141734)
XLA Ops:
  1.9 122.3 %shard_map.140 = (f32[256,128]{1,0:T(8,128)}, f32[16,8,128]{2,1,0:T(8,128)}) custom-call(s32[1]{0:T(128)S(6)} %copy.15.local_count, s32[1]{0:T(128)S(6)} %copy.16.remote_count, f32[256,128]{1,0:T(8,128)} %grad_hbm.1, bf16[256,128]{1,0:T(8,128)(2,1)} %phi_hbm.1, bf16[256,128]{1,0:T(8,128)(2,1)} %act_hbm.1, bf16[128,128]{1,0:T(8,128)(2,1)} %weight_hbm.1, ...), custom_call_target="tpu_custom_call" | custom-call | tf_op jit(solution)/shard_map/pallas_call | solution.py:500
  124.2 1.6 %shard_map.141 = (f32[256,128]{1,0:T(8,128)}, f32[128,128]{1,0:T(8,128)}) custom-call(f32[256,128]{1,0:T(8,128)} %get-tuple-element.4.adj_src, f32[128,128]{1,0:T(8,128)} %bitcast.8), custom_call_target="tpu_custom_call" | custom-call | tf_op jit(solution)/shard_map/pallas_call | solution.py:562

commit v5 on v4

--- a/solution.py
+++ b/solution.py
@@ -386,9 +386,17 @@
         layer(it, low)
         layer(it, lax.rem(low + 2, Z_LO))
         loop(count, arrived, self_k + 1)
-        layer(it, lax.rem(low + 1, Z_LO))
-        layer(it, lax.rem(low + 3, Z_LO))
-        adj_ref[...] = grad_ref[...] + GAMMA * total[...]
+        last = layer_blocks // span
+
+        def piece(i):
+            first = lax.rem(low + 1 + 2 * (i // last), Z_LO) * layer_blocks + i % last * span
+            source = halo[it, pl.ds(pl.multiple_of(first * tb, tb), span * tb), :]
+            return jnp.dot(tile_rows(1, halo_blocks, first, span), source, preferred_element_type=F32)
+
+        far = piece(0)
+        for i in range(1, 2 * last):
+            far += piece(i)
+        adj_ref[...] = grad_ref[...] + GAMMA * (total[...] + far)
 
         @pl.when(it < ITERS - 1)
         def _():
@@ -418,7 +426,7 @@
         other = lax.rem(me + k, plane)
         return share(part.at[other // CORES], plane_sum.at[me], (plane_send, plane_recv), k, device(z, other))
 
-    loop(plane, lambda k: plane_copy(k).start(), 1)
+    loop(plane - 1, lambda i: plane_copy(lax.rem(i + 3 * plane // 8, plane - 1) + 1).start())
     plane_sum[me] = part[chip]
     loop(plane, lambda k: plane_copy(k).wait_recv(), 1)
     column_sum[z] = jnp.sum(plane_sum[...], axis=0)
@@ -436,7 +444,8 @@
         where = device(z, chip_ahead(k) * CORES + core)
         return share(wg_all.at[chip], wg_all.at[chip], (last_send, last_recv), k, where)
 
-    loop(chips, lambda k: last_copy(k).start(), 1)
+    if chips > 1:
+        loop(chips - 1, lambda i: last_copy(lax.rem(i + 5 * chips // 16, chips - 1) + 1).start())
     loop(chips, lambda k: last_copy(k).wait_recv(), 1)
     wg_ref[...] = wg_all[...]
     loop(plane, lambda k: plane_copy(k).wait_send(), 1)

time: 126 us -> 125 us (level)
  no operation moved by 1% of the time
where the time goes in v5:
time: 125 us
  Pallas kernels  123 us (98%)
  between operations  1.93 us (2%)
    pallas_call x1, Pallas kernels, per_device(): pl.pallas_call(functools.partial(kernel, (plane, narrow, rows, tb, sendn,...  121 us

profile of v5, /device:TPU:1, one launch (start us, length us, event | category | flops | bytes accessed | tf_op | source)
XLA Modules:
  0.0 124.8 jit_solution(11744255873939776882)
XLA Ops:
  1.9 121.3 %shard_map.140 = (f32[256,128]{1,0:T(8,128)}, f32[16,8,128]{2,1,0:T(8,128)}) custom-call(s32[1]{0:T(128)S(6)} %copy.15.local_count, s32[1]{0:T(128)S(6)} %copy.16.remote_count, f32[256,128]{1,0:T(8,128)} %grad_hbm.1, bf16[256,128]{1,0:T(8,128)(2,1)} %phi_hbm.1, bf16[256,128]{1,0:T(8,128)(2,1)} %act_hbm.1, bf16[128,128]{1,0:T(8,128)(2,1)} %weight_hbm.1, ...), custom_call_target="tpu_custom_call" | custom-call | tf_op jit(solution)/shard_map/pallas_call | solution.py:509
  123.2 1.6 %shard_map.141 = (f32[256,128]{1,0:T(8,128)}, f32[128,128]{1,0:T(8,128)}) custom-call(f32[256,128]{1,0:T(8,128)} %get-tuple-element.4.adj_src, f32[128,128]{1,0:T(8,128)} %bitcast.8), custom_call_target="tpu_custom_call" | custom-call | tf_op jit(solution)/shard_map/pallas_call | solution.py:571
